TPU v7x, 512 devices: a whole 4x8x8 slice. The times are simulated.
512 devices in a mesh: dp: 32 (over x, z_lo, core), section: 8 (over y), mp: 2 (over z_hi).
Axes of the slice: x: 4, y: 8, z: 8 (z_hi: 2, z_lo: 4; z = z_hi * 4 + z_lo), core: 2. Of those that a mesh axis runs over, the one named last changes fastest.
Arguments:
- queries: bfloat16 [8, 4096, 2048], P('section', 'dp', 'mp'), may hold values from -45 to 45
- keys: bfloat16 [8, 8192, 2048], P('section', 'dp', 'mp'), may hold values from -6 to 6
- values: bfloat16 [8, 8192, 2048], P('section', 'dp', 'mp'), may hold values from -6 to 6
- out_grad: bfloat16 [8, 4096, 2048], P('section', 'dp', 'mp'), may hold values from -96 to 96
- key_weight: bfloat16 [8, 2048, 2048], P('section', 'dp', 'mp'), may hold values from -0.125 to 0.125
- encoded: bfloat16 [8192, 2048], P('dp', ('section', 'mp')), may hold values from -6 to 6
- enc_lengths: int32 [32], P('dp'), may hold values from 128 to 256
Outputs:
- query_grad: bfloat16 [8, 4096, 2048], P('section', 'dp', 'mp')
- encoder_grad: bfloat16 [8192, 2048], P('dp', ('section', 'mp'))
- weight_grad: float32 [8, 2048, 2048], P('section', 'dp', 'mp')
All inputs are finite; a program needn't handle non-finite values.
Results may differ from a plain program's by a relative error of at most 0.0058.
Values may be sent and summed in bfloat16 or wider, within the bound.
A program may use at most 64 MiB of HBM per device.

v0:
```python
import math

import jax
import jax.numpy as jnp
from jax import lax
from jax.sharding import PartitionSpec as P

HD = 256


NEG_FILL = -1e30


def heads_back(q, k, v, dout, length):
    dec_rows, width_all = q.shape
    enc_rows = k.shape[0]
    heads = width_all // HD
    group = math.gcd(heads, 8)
    width = group * HD
    scale = HD ** (-0.5)
    valid = (jnp.arange(enc_rows) < length)[None, None, :]

    def group_back(index):
        q_group = q.reshape(dec_rows, group, HD)
        k_group = k.reshape(enc_rows, group, HD)
        v_group = v.reshape(enc_rows, group, HD)
        d_group = dout.reshape(dec_rows, group, HD)
        scores = (
            jnp.einsum("qhd,khd->hqk", q_group, k_group, preferred_element_type=jnp.float32) * scale
        )
        scores = jnp.where(valid, scores, NEG_FILL)
        top = jnp.max(scores, axis=-1, keepdims=True)
        expo = jnp.exp(scores - top)
        probs = expo / jnp.sum(expo, axis=-1, keepdims=True)
        dprobs = jnp.einsum("qhd,khd->hqk", d_group, v_group, preferred_element_type=jnp.float32)
        delta = jnp.sum(probs * dprobs, axis=-1, keepdims=True)
        dscore = (probs * (dprobs - delta) * scale).astype(jnp.bfloat16)
        query_part = jnp.einsum("hqk,khd->qhd", dscore, k_group, preferred_element_type=jnp.float32)
        key_part = jnp.einsum("hqk,qhd->khd", dscore, q_group, preferred_element_type=jnp.float32)
        return (
            query_part.astype(jnp.bfloat16).reshape(dec_rows, width),
            key_part.astype(jnp.bfloat16).reshape(enc_rows, width),
        )

    query_parts, key_parts = lax.map(group_back, jnp.arange(heads // group))
    query_grad = jnp.transpose(query_parts, (1, 0, 2)).reshape(dec_rows, width_all)
    key_grad = jnp.transpose(key_parts, (1, 0, 2)).reshape(enc_rows, width_all)
    return (query_grad, key_grad)


def shards(queries, keys, values, out_grad, key_weight, encoded, enc_lengths):
    query_grad, key_grad = heads_back(queries[0], keys[0], values[0], out_grad[0], enc_lengths[0])
    weight_rows = key_weight[0]
    data_count = lax.axis_size("dp")
    term = jnp.dot(
        key_grad,
        lax.all_gather(weight_rows, "dp", axis=0, tiled=True).T,
        preferred_element_type=jnp.float32,
    )
    encoder_grad = lax.psum_scatter(
        term, ("section", "mp"), scatter_dimension=1, tiled=True
    ).astype(jnp.bfloat16)
    partial_grad = jnp.dot(
        lax.all_gather(encoded, ("section", "mp"), axis=1, tiled=True).T,
        key_grad,
        preferred_element_type=jnp.float32,
    )
    bucket = partial_grad.astype(jnp.bfloat16).reshape(
        data_count, partial_grad.shape[0] // data_count, partial_grad.shape[1]
    )
    received = lax.all_to_all(bucket, "dp", split_axis=0, concat_axis=0, tiled=True)
    weight_grad = (jnp.sum(received.astype(jnp.float32), axis=0) * (1.0 / data_count))[None]
    return (query_grad[None], encoder_grad, weight_grad)


def solution(mesh):
    placed = (
        P("section", "dp", "mp"),
        P("section", "dp", "mp"),
        P("section", "dp", "mp"),
        P("section", "dp", "mp"),
        P("section", "dp", "mp"),
        P("dp", ("section", "mp")),
        P("dp"),
    )
    return jax.shard_map(
        shards,
        mesh=mesh,
        in_specs=placed,
        out_specs=(P("section", "dp", "mp"), P("dp", ("section", "mp")), P("section", "dp", "mp")),
        check_vma=False,
    )
```

profile of v0, /device:TPU:1, one launch (start us, length us, event | category | flops | bytes accessed | tf_op | source)
XLA Modules:
  0.0 457.4 jit_solution(12095279228569412198)
XLA Ops:
  7.2 0.0 all-gather.4.cloned.1.call-start
  7.2 0.7 all-gather.4.cloned.1.call-update
  7.9 0.0 all-gather.6.cloned.1.call-start
  7.9 0.7 all-gather.6.cloned.1.call-update
  9.3 1.1 copy.25
  10.4 1.1 reshape_squeeze.18
  11.6 1.4 reshape_squeeze.17
  13.0 1.4 reshape_squeeze.19
  14.5 0.5 fusion.6
  15.0 0.3 fusion.18
  15.3 0.4 convolution_convert_fusion
  15.7 90.0 %all-gather.4.cloned.1.call-done = bf16[256,2048]{1,0:T(8,128)(2,1)} async-done(((bf16[256,128]{1,0:T(8,128)(2,1)}), bf16[256,2048]{1,0:T(8,128)(2,1)}) %all-gather.4.cloned.1.call-update) | async-done | bytes 1048592 | tf_op jit(solution)/shard_map/all_gather | solution.py:64
  105.7 4.5 convert_bitcast_fusion
  110.1 6.4 %copy.23 = bf16[2048,1024]{1,0:T(8,128)(2,1)} copy(bf16[2048,1024]{0,1:T(8,128)(2,1)} %convert_bitcast_fusion) | data formatting | bytes 8388608 | tf_op jit(solution)/shard_map/convert_element_type | solution.py:68
  116.5 9.3 %all-to-all-start = ((bf16[32,64,1024]{2,1,0:T(8,128)(2,1)}), bf16[32,64,1024]{2,1,0:T(8,128)(2,1)}, u32[]{:S(2)}, u32[]{:S(2)}) async-start(bf16[32,64,1024]{2,1,0:T(8,128)(2,1)} %bitcast.22), calls=%async_computation.1 | async-start | bytes 8388608 | tf_op jit(solution)/shard_map/all_to_all | solution.py:71
  125.8 0.0 reduce-scatter.2.cloned.1.call-start
  125.9 93.4 %all-gather.6.cloned.1.call-done = bf16[1,2048,1024]{2,1,0:T(8,128)(2,1)} async-done(((bf16[1,64,1024]{2,1,0:T(8,128)(2,1)}), bf16[1,2048,1024]{2,1,0:T(8,128)(2,1)}) %all-gather.6.cloned.1.call-update) | async-done | bytes 4194320 | tf_op jit(solution)/shard_map/all_gather | solution.py:57
  219.3 4.8 %fusion.3 = f32[256,2048]{1,0:T(8,128)} fusion(bf16[256,1024]{0,1:T(8,128)(2,1)S(1)} %bitcast.24, bf16[1,2048,1024]{2,1,0:T(8,128)(2,1)} %all-gather.6.cloned.1.call-done), kind=kOutput, calls=%fused_computation.4 | convolution fusion | flops 1073741824 | bytes 6815744 | tf_op jit(solution)/shard_map/dot_general | solution.py:55
  224.2 0.0 reduce-scatter.2.cloned.1.call-update
  224.2 0.3 fusion.13
  224.5 0.2 copy.21
  224.6 0.9 copy.24
  225.5 12.3 %all-to-all-done = bf16[32,64,1024]{2,1,0:T(8,128)(2,1)} async-done(((bf16[32,64,1024]{2,1,0:T(8,128)(2,1)}), bf16[32,64,1024]{2,1,0:T(8,128)(2,1)}, u32[]{:S(2)}, u32[]{:S(2)}) %all-to-all-start) | async-done | bytes 4194336 | tf_op jit(solution)/shard_map/all_to_all | solution.py:71
  237.8 3.1 convert_reduce_fusion
  240.9 0.7 multiply_bitcast_fusion
  241.7 207.6 %reduce-scatter.2.cloned.1.call-done = f32[256,128]{1,0:T(8,128)} async-done(((f32[256,2048]{1,0:T(8,128)}), f32[256,128]{1,0:T(8,128)}) %reduce-scatter.2.cloned.1.call-update) | async-done | bytes 131088 | tf_op jit(solution)/shard_map/reduce_scatter | solution.py:60
  449.3 1.5 convert_element_type.35
  (1 shorter events, 0.0 us)
Async XLA Ops:
  7.2 98.5 %all-gather.4.cloned.1.call-start = ((), (), s32[]{:S(2)}) async-start(), calls=%async_computation.3 | async-start | bytes 1114112 | tf_op jit(solution)/shard_map/all_gather | solution.py:64
  7.9 211.4 %all-gather.6.cloned.1.call-start = ((), (), s32[]{:S(2)}) async-start(), calls=%async_computation.4 | async-start | bytes 4325376 | tf_op jit(solution)/shard_map/all_gather | solution.py:57
  116.5 121.3 %all-to-all-start = ((bf16[32,64,1024]{2,1,0:T(8,128)(2,1)}), bf16[32,64,1024]{2,1,0:T(8,128)(2,1)}, u32[]{:S(2)}, u32[]{:S(2)}) async-start(bf16[32,64,1024]{2,1,0:T(8,128)(2,1)} %bitcast.22), calls=%async_computation.1 | async-start | bytes 8388608 | tf_op jit(solution)/shard_map/all_to_all | solution.py:71
  125.8 323.5 %reduce-scatter.2.cloned.1.call-start = ((), (), s32[]{:S(2)}) async-start(), calls=%async_computation.2 | async-start | bytes 2228224 | tf_op jit(solution)/shard_map/reduce_scatter | solution.py:60
Sparse Core Ops, SparseCore 0:
  11.1 94.5 all-gather.3
  107.8 111.4 all-gather.5
  224.3 224.9 reduce-scatter.1
where the time goes:
time: 462 us; the launch traced here: 457 us
  waiting for transfers between devices  405 us (88%)
  between operations  14.5 us (3%)
  local copies, waits for them, and re-layouts  12.6 us (3%)
  matrix products  10.8 us (2%)
  starting transfers between devices  9.43 us (2%)
  other arithmetic  5.41 us (1%)
    reduce_scatter x1, waiting for transfers between devices, shards(): lax.psum_scatter(term, ('section', 'mp'), scatter_dimension=1, tiled=True)  208 us
    all_gather x1, waiting for transfers between devices, shards(): lax.all_gather(weight_rows, 'dp', axis=0, tiled=True)  93.4 us
    all_gather x1, waiting for transfers between devices, shards(): lax.all_gather(encoded, ('section', 'mp'), axis=1, tiled=True)  90 us
    all_to_all x1, waiting for transfers between devices, shards(): lax.all_to_all(bucket, 'dp', split_axis=0, concat_axis=0, tiled=True)  12.3 us
    all_to_all x1, starting transfers between devices, shards(): lax.all_to_all(bucket, 'dp', split_axis=0, concat_axis=0, tiled=True)  9.32 us
  transfers between devices with their start and end apart: 4, of which 4 were waited for; matrix products, arithmetic and copies ran while one was open for 6% of the time, Pallas kernels for 0%

commit v1 on v0

v1 whole, which is shorter than its diff:
```python
import jax
import jax.numpy as jnp
from jax import lax
from jax.experimental import pallas as pl
from jax.experimental.pallas import tpu as pltpu
from jax.sharding import PartitionSpec as P

HD = 256
NEG_FILL = -1e30
X, Z, Y = 4, 4, 8
F = X * Z
MESH = pl.DeviceIdType.MESH
BF = jnp.bfloat16
F32 = jnp.float32

NT = (((1,), (1,)), ((), ()))
NN = (((1,), (0,)), ((), ()))
TN = (((0,), (0,)), ((), ()))


def dot(a, b, dims):
    return lax.dot_general(a, b, dims, preferred_element_type=F32)


def kernel(
    q_hbm, k_hbm, v_hbm, d_hbm, w_hbm, enc_hbm, len_ref,
    qg_ref, eg_ref, wg_ref,
    q_v, k_v, v_v, d_v, enc_v, et, ebuf, wbuf, kg,
    term, e_send, e_recv, e_last, fin, enc_sum,
    part, a_send, a_recv, b_send, b_recv, z_send, z_recv,
    loc_sem, ws_sem, wr_sem, es_sem, er_sem, ks_sem, kr_sem,
    ts_sem, tr_sem, ls_sem, lr_sem, as_sem, ar_sem, bs_sem, br_sem, zs_sem, zr_sem,
):
    dp = lax.axis_index("dp")
    y = lax.axis_index("section")
    m = lax.axis_index("mp")
    x = dp // 8
    z = (dp // 2) % 4
    c = dp % 2
    f = dp // 2
    g = y * 2 + m

    def dev(x=x, z=z, c=c, y=y, m=m):
        return {"dp": x * 8 + z * 2 + c, "section": y, "mp": m}

    x_up, x_down = (x + 1) % X, (x + X - 1) % X
    y_up, y_down = (y + 1) % Y, (y + Y - 1) % Y
    sister, m_other = 1 - c, 1 - m
    dev_xu, dev_xd = dev(x=x_up), dev(x=x_down)
    dev_yu, dev_yd = dev(y=y_up), dev(y=y_down)
    dev_z = [None] + [dev(z=(z + dz) % Z) for dz in range(1, Z)]
    dev_s, dev_m, dev_ms = dev(c=sister), dev(m=m_other), dev(c=sister, m=m_other)

    partners = [dev_xu, dev_xd, dev_yu, dev_yd] + dev_z[1:] + [dev_s, dev_m, dev_ms]
    barrier = pltpu.get_barrier_semaphore()
    for partner in partners:
        pl.semaphore_signal(barrier, inc=1, device_id=partner, device_id_type=MESH)

    locals_ = [
        pltpu.make_async_copy(src, dst, loc_sem.at[i])
        for i, (src, dst) in enumerate(
            [(enc_hbm, enc_v), (q_hbm, q_v), (k_hbm, k_v), (d_hbm, d_v), (v_hbm, v_v), (w_hbm, wbuf.at[f])]
        )
    ]
    for copy in locals_:
        copy.start()
    pl.semaphore_wait(barrier, len(partners))

    sent = []

    def send(src, dst, ssem, rsem, device):
        copy = pltpu.make_async_remote_copy(
            src_ref=src, dst_ref=dst, send_sem=ssem, recv_sem=rsem, device_id=device, device_id_type=MESH
        )
        copy.start()
        sent.append(copy)
        return copy

    arrived = set()

    def arrive(inward, key):
        if (id(inward), key) not in arrived:
            arrived.add((id(inward), key))
            inward[key].wait_recv()

    w_in = {}
    w_in[(3, 0)] = send(w_hbm, wbuf.at[f], ws_sem.at[0], wr_sem.at[12], dev_xu)
    w_in[(1, 0)] = send(w_hbm, wbuf.at[f], ws_sem.at[1], wr_sem.at[4], dev_xd)
    for dz in (1, 3, 2):
        back = (Z - dz) % Z
        w_in[(0, back)] = send(w_hbm, wbuf.at[f], ws_sem.at[1 + dz], wr_sem.at[back], dev_z[dz])

    def w_column(dz):
        arrive(w_in, (0, dz))
        slot = x * Z + (z + dz) % Z
        w_in[(3, dz)] = send(wbuf.at[slot], wbuf.at[slot], ws_sem.at[4 + dz], wr_sem.at[12 + dz], dev_xu)
        w_in[(1, dz)] = send(wbuf.at[slot], wbuf.at[slot], ws_sem.at[7 + dz], wr_sem.at[4 + dz], dev_xd)

    def w_far(dz):
        if dz < 2:
            arrive(w_in, (3, dz))
            slot = x_down * Z + (z + dz) % Z
            to = dev_xu
        else:
            arrive(w_in, (1, dz))
            slot = x_up * Z + (z + dz) % Z
            to = dev_xd
        w_in[(2, dz)] = send(wbuf.at[slot], wbuf.at[slot], ws_sem.at[11 + dz], wr_sem.at[8 + dz], to)

    locals_[0].wait()
    enc_t = enc_v[...].astype(F32).T.astype(BF)
    et[0] = enc_t[:64]
    et[1] = enc_t[64:]
    ebuf[g, :, 0:256] = et[c]
    e_pair = send(et.at[sister], ebuf.at[g, :, pl.ds(256, 256)], es_sem.at[0], er_sem.at[16], dev_s)
    e_in = {}

    def e_out(up, dy, dm):
        slot = ((y + dy) % Y) * 2 + (m_other if dm else m)
        if up:
            there = (dy + Y - 1) % Y
            number = 2 + ((Y - dy) % Y) * 2 + dm
        else:
            there = dy + 1
            number = 10 + dy * 2 + dm
        e_in[(there, dm)] = send(
            ebuf.at[slot], ebuf.at[slot], es_sem.at[number], er_sem.at[there * 2 + dm], dev_yu if up else dev_yd
        )

    def e_own():
        e_pair.wait_recv()
        e_in[(0, 1)] = send(ebuf.at[g], ebuf.at[g], es_sem.at[1], er_sem.at[1], dev_m)
        e_out(True, 0, 0)
        e_out(False, 0, 0)

    def e_other():
        arrive(e_in, (0, 1))
        e_out(True, 0, 1)
        e_out(False, 0, 1)

    def e_step(k, dm):
        if k < 3 or dm == 0:
            arrive(e_in, (Y - k, dm))
            e_out(True, Y - k, dm)
        if k < 3 or dm == 1:
            arrive(e_in, (k, dm))
            e_out(False, k, dm)

    scale = HD ** (-0.5)
    length = len_ref[0]
    valid = lax.broadcasted_iota(jnp.int32, (128, 256), 1) < length

    def head(h):
        cols = slice(h * HD, (h + 1) * HD)
        qh, kh, vh, dh = q_v[:, cols], k_v[:, cols], v_v[:, cols], d_v[:, cols]
        scores = dot(qh, kh, NT) * scale
        scores = jnp.where(valid, scores, NEG_FILL)
        top = jnp.max(scores, axis=-1, keepdims=True)
        expo = jnp.exp(scores - top)
        probs = expo / jnp.sum(expo, axis=-1, keepdims=True)
        dprobs = dot(dh, vh, NT)
        delta = jnp.sum(probs * dprobs, axis=-1, keepdims=True)
        dscore = probs * (dprobs - delta) * scale
        qg_ref[:, cols] = dot(dscore.astype(BF), kh, NN).astype(BF)
        kg[0, :, cols] = dot(dscore.T.astype(BF), qh, NN).astype(BF)

    locals_[1].wait()
    locals_[2].wait()
    locals_[3].wait()
    locals_[4].wait()
    head(0)
    e_own()
    head(1)
    w_column(1)
    head(2)
    w_column(3)
    head(3)
    k_pair = send(kg.at[0], kg.at[1], ks_sem.at[0], kr_sem.at[0], dev_s)
    e_other()
    e_step(1, 0)
    w_far(0)
    w_column(2)
    e_step(1, 1)
    e_step(2, 0)
    w_far(1)
    w_far(3)
    e_step(2, 1)
    e_step(3, 0)
    w_far(2)
    e_step(3, 1)

    k_pair.wait_recv()
    for key in sorted(e_in):
        arrive(e_in, key)

    grads = kg[...].reshape(512, 1024)

    def wg_dot(xt):
        rows = ebuf[pl.ds(xt * Z, Z)].reshape(256, 512)
        part[pl.ds(xt * Z, Z)] = dot(rows, grads, NN).reshape(Z, 64, 1024)

    x_far = (x + 2) % X
    wg_dot(x_far)
    a_in, b_in = {}, {}
    for up in (1, 0):
        for j in range(2):
            zt = j if up else 2 + j
            a_send[up, j] = part[x_far * Z + zt].astype(BF)
            a_in[(up, j)] = send(
                a_send.at[up, j], a_recv.at[up, j], as_sem.at[up * 2 + j], ar_sem.at[up * 2 + j],
                dev_xu if up else dev_xd,
            )

    def b_out(up, zt, value):
        b_send[up, zt] = value.astype(BF)
        b_in[(up, zt)] = send(
            b_send.at[up, zt], b_recv.at[up, zt], bs_sem.at[up * 4 + zt], br_sem.at[up * 4 + zt],
            dev_xu if up else dev_xd,
        )

    wg_dot(x_up)
    for zt in (2, 3):
        b_out(1, zt, part[x_up * Z + zt])
    wg_dot(x_down)
    for zt in (0, 1):
        b_out(0, zt, part[x_down * Z + zt])
    wg_dot(x)

    locals_[5].wait()
    for key in sorted(w_in):
        arrive(w_in, key)

    def eg_dot(yt):
        rows = wbuf[pl.ds(yt * 2, 2)].reshape(128, 1024)
        term[pl.ds(yt * 2, 2)] = dot(rows, grads, NT).reshape(2, 64, 512)

    t_in = {}

    def t_out(up, k, half):
        yt = (y + k) % Y if up else (y + Y - k) % Y
        value = term[yt * 2 + half]
        first = 4 if half != up else 3
        if k < first:
            arrive(t_in, (up, k + 1, half))
            value = value + e_recv[up, k, half].astype(F32)
        e_send[up, k - 1, half] = value.astype(BF)
        number = (up * 4 + k - 1) * 2 + half
        t_in[(up, k, half)] = send(
            e_send.at[up, k - 1, half], e_recv.at[up, k - 1, half], ts_sem.at[number], tr_sem.at[number],
            dev_yu if up else dev_yd,
        )

    eg_dot((y + 4) % Y)
    t_out(1, 4, 0)
    t_out(0, 4, 1)
    eg_dot((y + 3) % Y)
    t_out(1, 3, 1)
    eg_dot((y + 5) % Y)
    t_out(0, 3, 0)
    eg_dot((y + 2) % Y)
    eg_dot((y + 6) % Y)

    def b_sum(up, j):
        zt = j if up else 2 + j
        arrive(a_in, (up, j))
        b_out(up, zt, part[(x_up if up else x_down) * Z + zt] + a_recv[up, j].astype(F32))

    b_sum(1, 0)
    b_sum(0, 0)
    t_out(1, 3, 0)
    t_out(0, 3, 1)
    eg_dot((y + 1) % Y)
    eg_dot((y + 7) % Y)
    b_sum(1, 1)
    b_sum(0, 1)
    t_out(1, 2, 1)
    t_out(0, 2, 0)
    eg_dot(y)
    t_out(1, 2, 0)
    t_out(0, 2, 1)
    t_out(1, 1, 1)
    t_out(0, 1, 0)
    t_out(1, 1, 0)
    t_out(0, 1, 1)

    for up in (1, 0):
        for zt in range(Z):
            arrive(b_in, (up, zt))

    def x_sum(zt):
        return part[x * Z + zt] + b_recv[1, zt].astype(F32) + b_recv[0, zt].astype(F32)

    z_in = {}
    for dz in (2, 1, 3):
        zt = (z + dz) % Z
        z_send[dz - 1] = x_sum(zt).astype(BF)
        back = Z - dz
        z_in[back] = send(z_send.at[dz - 1], z_recv.at[back - 1], zs_sem.at[dz - 1], zr_sem.at[back - 1], dev_z[dz])
    own = x_sum(z)

    for up in (1, 0):
        for half in range(2):
            arrive(t_in, (up, 1, half))

    def y_sum(half):
        return term[y * 2 + half] + e_recv[1, 0, half].astype(F32) + e_recv[0, 0, half].astype(F32)

    away = y_sum(m_other).astype(BF)
    e_last[0] = away[:, 0:256]
    e_last[1] = away[:, 256:512]
    l_in = [
        send(e_last.at[0], fin.at[0], ls_sem.at[0], lr_sem.at[0], dev_m),
        send(e_last.at[1], fin.at[1], ls_sem.at[1], lr_sem.at[1], dev_ms),
    ]
    home = y_sum(m)
    e_last[2] = home[:, 256:512].astype(BF)
    l_in.append(send(e_last.at[2], fin.at[2], ls_sem.at[2], lr_sem.at[2], dev_s))

    for back in (2, 1, 3):
        arrive(z_in, back)
    own = own + z_recv[0].astype(F32) + z_recv[1].astype(F32) + z_recv[2].astype(F32)
    wg_ref[...] = own * (1.0 / 32)

    for copy in l_in:
        copy.wait_recv()
    enc_sum[c] = home[:, 0:256] + fin[0].astype(F32)
    enc_sum[sister] = fin[1].astype(F32) + fin[2].astype(F32)
    eg_ref[...] = enc_sum[...].reshape(128, 256).T.astype(BF)

    for copy in sent:
        copy.wait_send()


def shards(queries, keys, values, out_grad, key_weight, encoded, enc_lengths):
    dma = pltpu.SemaphoreType.DMA
    anywhere = pl.BlockSpec(memory_space=pl.ANY)
    vmem = pl.BlockSpec(memory_space=pltpu.VMEM)
    query_grad, encoder_grad, weight_grad = pl.pallas_call(
        kernel,
        out_shape=(
            jax.ShapeDtypeStruct((128, 1024), BF),
            jax.ShapeDtypeStruct((256, 128), BF),
            jax.ShapeDtypeStruct((64, 1024), F32),
        ),
        in_specs=[anywhere] * 6 + [pl.BlockSpec(memory_space=pltpu.SMEM)],
        out_specs=(vmem, vmem, vmem),
        scratch_shapes=[
            pltpu.VMEM((128, 1024), BF),
            pltpu.VMEM((256, 1024), BF),
            pltpu.VMEM((256, 1024), BF),
            pltpu.VMEM((128, 1024), BF),
            pltpu.VMEM((256, 128), BF),
            pltpu.VMEM((2, 64, 256), BF),
            pltpu.VMEM((F, 64, 512), BF),
            pltpu.VMEM((F, 64, 1024), BF),
            pltpu.VMEM((2, 256, 1024), BF),
            pltpu.VMEM((F, 64, 512), F32),
            pltpu.VMEM((2, 4, 2, 64, 512), BF),
            pltpu.VMEM((2, 4, 2, 64, 512), BF),
            pltpu.VMEM((3, 64, 256), BF),
            pltpu.VMEM((3, 64, 256), BF),
            pltpu.VMEM((2, 64, 256), F32),
            pltpu.VMEM((F, 64, 1024), F32),
            pltpu.VMEM((2, 2, 64, 1024), BF),
            pltpu.VMEM((2, 2, 64, 1024), BF),
            pltpu.VMEM((2, 4, 64, 1024), BF),
            pltpu.VMEM((2, 4, 64, 1024), BF),
            pltpu.VMEM((3, 64, 1024), BF),
            pltpu.VMEM((3, 64, 1024), BF),
            dma((6,)), dma((15,)), dma((16,)), dma((18,)), dma((17,)), dma((1,)), dma((1,)),
            dma((16,)), dma((16,)), dma((3,)), dma((3,)), dma((4,)), dma((4,)), dma((8,)), dma((8,)),
            dma((3,)), dma((3,)),
        ],
        compiler_params=pltpu.CompilerParams(
            collective_id=0, has_side_effects=True, vmem_limit_bytes=48 * 1024 * 1024
        ),
    )(queries[0], keys[0], values[0], out_grad[0], key_weight[0], encoded, enc_lengths)
    return (query_grad[None], encoder_grad, weight_grad[None])


def solution(mesh):
    placed = (
        P("section", "dp", "mp"),
        P("section", "dp", "mp"),
        P("section", "dp", "mp"),
        P("section", "dp", "mp"),
        P("section", "dp", "mp"),
        P("dp", ("section", "mp")),
        P("dp"),
    )
    return jax.shard_map(
        shards,
        mesh=mesh,
        in_specs=placed,
        out_specs=(P("section", "dp", "mp"), P("dp", ("section", "mp")), P("section", "dp", "mp")),
        check_vma=False,
    )
```

time: 462 us -> 82 us (0.18)
  waiting for transfers between devices: 405 us -> 0 us
  Pallas kernels: 0 us -> 71.9 us
  between operations: 14.5 us -> 1.3 us
  matrix products: 10.8 us -> 0 us
  starting transfers between devices: 9.43 us -> 0 us
  other arithmetic: 5.41 us -> 0 us
  local copies, waits for them, and re-layouts: 12.6 us -> 7.75 us
    reduce_scatter x1 -> x0, waiting for transfers between devices: 208 us -> none  [shards(): lax.psum_scatter(term, ('section', 'mp'), scatter_dimension=1, tiled=True)]
    all_gather x2 -> x0, waiting for transfers between devices: 183 us -> none  [the longest x1 93.4 us: shards(): lax.all_gather(weight_rows, 'dp', axis=0, tiled=True)]
    pallas_call x0 -> x1, Pallas kernels: none -> 71.9 us  [shards(): pl.pallas_call(kernel, out_shape=(jax.ShapeDtypeStruct((128, 1024), BF),...]
    all_to_all x1 -> x0, waiting for transfers between devices: 12.3 us -> none  [shards(): lax.all_to_all(bucket, 'dp', split_axis=0, concat_axis=0, tiled=True)]
    dot_general x5 -> x0, matrix products: 10.3 us -> none  [the longest x1 4.85 us: shards(): jnp.dot(key_grad, lax.all_gather(weight_rows, 'dp', axis=0, tiled=True).T...]
    all_to_all x1 -> x0, starting transfers between devices: 9.32 us -> none  [shards(): lax.all_to_all(bucket, 'dp', split_axis=0, concat_axis=0, tiled=True)]
    unnamed x1 -> x15, local copies, waits for them, and re-layouts: 0.85 us -> 7.75 us
    convert_element_type x2 -> x0, local copies, waits for them, and re-layouts: 6.57 us -> none  [the longest x1 6.4 us: shards(): partial_grad.astype(jnp.bfloat16)]
  transfers between devices with their start and end apart: 4 -> 0, of which waited for: 4 -> 0; matrix products, arithmetic and copies ran while one was open for 6% -> 0% of each run, Pallas kernels for 0% -> 0%
where the time goes in v1:
time: 82 us; the launch traced here: 81 us
  Pallas kernels  71.9 us (88%)
  local copies, waits for them, and re-layouts  7.75 us (9%)
  between operations  1.3 us (2%)
    pallas_call x1, Pallas kernels, shards(): pl.pallas_call(kernel, out_shape=(jax.ShapeDtypeStruct((128, 1024), BF),...  71.9 us
    unnamed x15, local copies, waits for them, and re-layouts  7.75 us

profile of v1, /device:TPU:1, one launch (start us, length us, event | category | flops | bytes accessed | tf_op | source)
XLA Modules:
  0.0 81.0 jit_solution(3682210408572279883)
XLA Ops:
  1.3 0.0 copy-start
  1.3 1.0 %copy-done = bf16[1,256,1024]{2,1,0:T(8,128)(2,1)S(1)} copy-done((bf16[1,256,1024]{2,1,0:T(8,128)(2,1)S(1)}, bf16[1,256,1024]{2,1,0:T(8,128)(2,1)}, u32[]{:S(2)}) %copy-start) | copy-done | bytes 524312
  2.3 0.0 copy-start.1
  2.3 1.0 %copy-done.1 = bf16[1,256,1024]{2,1,0:T(8,128)(2,1)S(1)} copy-done((bf16[1,256,1024]{2,1,0:T(8,128)(2,1)S(1)}, bf16[1,256,1024]{2,1,0:T(8,128)(2,1)}, u32[]{:S(2)}) %copy-start.1) | copy-done | bytes 524312
  3.4 0.0 copy-start.2
  3.4 0.9 %copy-done.2 = bf16[1,128,1024]{2,1,0:T(8,128)(2,1)S(1)} copy-done((bf16[1,128,1024]{2,1,0:T(8,128)(2,1)S(1)}, bf16[1,128,1024]{2,1,0:T(8,128)(2,1)}, u32[]{:S(2)}) %copy-start.2) | copy-done | bytes 262168
  4.3 0.0 copy-start.3
  4.3 0.9 %copy-done.3 = bf16[1,128,1024]{2,1,0:T(8,128)(2,1)S(1)} copy-done((bf16[1,128,1024]{2,1,0:T(8,128)(2,1)S(1)}, bf16[1,128,1024]{2,1,0:T(8,128)(2,1)}, u32[]{:S(2)}) %copy-start.3) | copy-done | bytes 262168
  5.3 0.0 copy-start.4
  5.3 0.9 %copy-done.4 = bf16[1,64,1024]{2,1,0:T(8,128)(2,1)S(1)} copy-done((bf16[1,64,1024]{2,1,0:T(8,128)(2,1)S(1)}, bf16[1,64,1024]{2,1,0:T(8,128)(2,1)}, u32[]{:S(2)}) %copy-start.4) | copy-done | bytes 131096
  6.2 0.0 copy-start.5
  6.2 0.8 %copy-done.5 = bf16[256,128]{1,0:T(8,128)(2,1)S(1)} copy-done((bf16[256,128]{1,0:T(8,128)(2,1)S(1)}, bf16[256,128]{1,0:T(8,128)(2,1)}, u32[]{:S(2)}) %copy-start.5) | copy-done | bytes 65560
  7.0 71.9 %shard_map.94 = (bf16[128,1024]{1,0:T(8,128)(2,1)S(1)}, bf16[256,128]{1,0:T(8,128)(2,1)S(1)}, f32[64,1024]{1,0:T(8,128)S(1)}) custom-call(bf16[128,1024]{1,0:T(8,128)(2,1)S(1)} %bitcast.11, bf16[256,1024]{1,0:T(8,128)(2,1)S(1)} %bitcast.7, bf16[256,1024]{1,0:T(8,128)(2,1)S(1)} %bitcast.8, bf16[128,1024]{1,0:T(8,128)(2,1)S(1)} %bitcast.12, ...), custom_call_target="tpu_custom_call" | custom-call | tf_op jit(solution)/shard_map/pallas_call | solution.py:338
  78.9 0.7 copy.14
  79.6 0.6 copy.15
  80.3 0.7 copy.16
Async XLA Ops:
  1.3 1.0 %copy-start = (bf16[1,256,1024]{2,1,0:T(8,128)(2,1)S(1)}, bf16[1,256,1024]{2,1,0:T(8,128)(2,1)}, u32[]{:S(2)}) copy-start(bf16[1,256,1024]{2,1,0:T(8,128)(2,1)} %param.8) | copy-start | bytes 1572868
  2.3 1.0 %copy-start.1 = (bf16[1,256,1024]{2,1,0:T(8,128)(2,1)S(1)}, bf16[1,256,1024]{2,1,0:T(8,128)(2,1)}, u32[]{:S(2)}) copy-start(bf16[1,256,1024]{2,1,0:T(8,128)(2,1)} %param.9) | copy-start | bytes 1572868
  3.4 0.9 %copy-start.2 = (bf16[1,128,1024]{2,1,0:T(8,128)(2,1)S(1)}, bf16[1,128,1024]{2,1,0:T(8,128)(2,1)}, u32[]{:S(2)}) copy-start(bf16[1,128,1024]{2,1,0:T(8,128)(2,1)} %param.7) | copy-start | bytes 786436
  4.3 0.9 %copy-start.3 = (bf16[1,128,1024]{2,1,0:T(8,128)(2,1)S(1)}, bf16[1,128,1024]{2,1,0:T(8,128)(2,1)}, u32[]{:S(2)}) copy-start(bf16[1,128,1024]{2,1,0:T(8,128)(2,1)} %param.10) | copy-start | bytes 786436
  5.3 0.9 %copy-start.4 = (bf16[1,64,1024]{2,1,0:T(8,128)(2,1)S(1)}, bf16[1,64,1024]{2,1,0:T(8,128)(2,1)}, u32[]{:S(2)}) copy-start(bf16[1,64,1024]{2,1,0:T(8,128)(2,1)} %param.11) | copy-start | bytes 393220
  6.2 0.8 %copy-start.5 = (bf16[256,128]{1,0:T(8,128)(2,1)S(1)}, bf16[256,128]{1,0:T(8,128)(2,1)}, u32[]{:S(2)}) copy-start(bf16[256,128]{1,0:T(8,128)(2,1)} %enc_hbm.1) | copy-start | bytes 196612

commit v2 on v1

v2 whole, which is shorter than its diff:
```python
import jax
import jax.numpy as jnp
from jax import lax
from jax.experimental import pallas as pl
from jax.experimental.pallas import tpu as pltpu
from jax.sharding import PartitionSpec as P

HD = 256
NEG_FILL = -1e30
X, Z, Y = 4, 4, 8
F = X * Z
MESH = pl.DeviceIdType.MESH
BF = jnp.bfloat16
F32 = jnp.float32

NT = (((1,), (1,)), ((), ()))
NN = (((1,), (0,)), ((), ()))
TN = (((0,), (0,)), ((), ()))


def dot(a, b, dims):
    return lax.dot_general(a, b, dims, preferred_element_type=F32)


def kernel(
    q_hbm, k_hbm, v_hbm, d_hbm, w_hbm, enc_hbm, len_hbm,
    qg_ref, eg_ref, wg_ref,
    q_v, k_v, v_v, d_v, enc_v, len_ref, et, ebuf, wbuf, kg,
    term, e_send, e_recv, e_last, fin, enc_sum,
    part, a_send, a_recv, b_send, b_recv, z_send, z_recv,
    loc_sem, ws_sem, wr_sem, es_sem, er_sem, ks_sem, kr_sem,
    ts_sem, tr_sem, ls_sem, lr_sem, as_sem, ar_sem, bs_sem, br_sem, zs_sem, zr_sem,
):
    dp = lax.axis_index("dp")
    y = lax.axis_index("section")
    m = lax.axis_index("mp")
    x = dp // 8
    z = (dp // 2) % 4
    c = dp % 2
    f = dp // 2
    g = y * 2 + m

    def dev(x=x, z=z, c=c, y=y, m=m):
        return {"dp": x * 8 + z * 2 + c, "section": y, "mp": m}

    x_up, x_down = (x + 1) % X, (x + X - 1) % X
    y_up, y_down = (y + 1) % Y, (y + Y - 1) % Y
    sister, m_other = 1 - c, 1 - m
    dev_xu, dev_xd, dev_x2 = dev(x=x_up), dev(x=x_down), dev(x=(x + 2) % X)
    dev_yu, dev_yd = dev(y=y_up), dev(y=y_down)
    dev_yu2, dev_yd2 = dev(y=(y + 2) % Y), dev(y=(y + Y - 2) % Y)
    z_other = [z, z + 1 - 2 * (z % 2), (z + 2) % Z, Z - 1 - z]
    dev_z = [dev(z=other) for other in z_other]
    dev_s, dev_m, dev_ms = dev(c=sister), dev(m=m_other), dev(c=sister, m=m_other)

    loads = [
        pltpu.make_async_copy(src, dst, loc_sem.at[i])
        for i, (src, dst) in enumerate(
            [(enc_hbm, enc_v), (q_hbm, q_v), (k_hbm, k_v), (d_hbm, d_v), (v_hbm, v_v), (w_hbm, wbuf.at[f]),
             (len_hbm, len_ref)]
        )
    ]

    partners = [dev_xu, dev_xd, dev_x2, dev_yu, dev_yd, dev_yu2, dev_yd2] + dev_z[1:] + [dev_s, dev_m, dev_ms]
    barrier = pltpu.get_barrier_semaphore()
    for partner in partners:
        pl.semaphore_signal(barrier, inc=1, device_id=partner, device_id_type=MESH)
    for copy in loads:
        copy.start()
    loads[0].wait()
    enc_t = enc_v[...].astype(F32).T.astype(BF)
    et[0] = enc_t[:64]
    et[1] = enc_t[64:]
    ebuf[g, :, 0:256] = et[c]
    pl.semaphore_wait(barrier, len(partners))

    sent = []

    def send(src, dst, ssem, rsem, device):
        copy = pltpu.make_async_remote_copy(
            src_ref=src, dst_ref=dst, send_sem=ssem, recv_sem=rsem, device_id=device, device_id_type=MESH
        )
        copy.start()
        sent.append(copy)
        return copy

    arrived = set()

    def arrive(inward, key):
        if (id(inward), key) not in arrived:
            arrived.add((id(inward), key))
            inward[key].wait_recv()

    e_in, w_in = {}, {}
    e_in["mine"] = send(et.at[sister], ebuf.at[g, :, pl.ds(256, 256)], es_sem.at[0], er_sem.at[0], dev_s)
    e_in["same"] = send(et.at[c], ebuf.at[g, :, pl.ds(0, 256)], es_sem.at[1], er_sem.at[1], dev_m)
    e_in["cross"] = send(et.at[sister], ebuf.at[g, :, pl.ds(256, 256)], es_sem.at[16], er_sem.at[16], dev_ms)

    w_in[(3, 0)] = send(w_hbm, wbuf.at[f], ws_sem.at[0], wr_sem.at[12], dev_xu)
    w_in[(1, 0)] = send(w_hbm, wbuf.at[f], ws_sem.at[1], wr_sem.at[4], dev_xd)
    for k in (1, 3):
        w_in[(0, k)] = send(w_hbm, wbuf.at[f], ws_sem.at[1 + k], wr_sem.at[k], dev_z[k])
    w_in[(2, 0)] = send(w_hbm, wbuf.at[f], ws_sem.at[3], wr_sem.at[8], dev_x2)

    inner = z * (3 - z) > 0

    def w_relay(k):
        arrive(w_in, (0, k))
        slot = x * Z + z_other[k]
        copy = pltpu.make_async_remote_copy(
            src_ref=wbuf.at[slot], dst_ref=wbuf.at[slot], send_sem=ws_sem.at[18 + k // 2], recv_sem=wr_sem.at[2],
            device_id=dev_z[4 - k], device_id_type=MESH,
        )
        w_in[(0, 2)] = copy
        relayed.append(copy)

        @pl.when(inner)
        def _():
            copy.start()

    relayed = []

    def w_column(k):
        arrive(w_in, (0, k))
        slot = x * Z + z_other[k]
        w_in[(3, k)] = send(wbuf.at[slot], wbuf.at[slot], ws_sem.at[4 + k], wr_sem.at[12 + k], dev_xu)
        w_in[(1, k)] = send(wbuf.at[slot], wbuf.at[slot], ws_sem.at[7 + k], wr_sem.at[4 + k], dev_xd)

    def w_far(k):
        arrive(w_in, (3, k))
        half = wbuf.at[x_down * Z + z_other[k], pl.ds(0, 32)]
        w_in[(2, k)] = send(half, half, ws_sem.at[10 + k], wr_sem.at[8 + k], dev_xu)
        arrive(w_in, (1, k))
        half = wbuf.at[x_up * Z + z_other[k], pl.ds(32, 32)]
        w_in[(6, k)] = send(half, half, ws_sem.at[13 + k], wr_sem.at[16 + k], dev_xd)

    def e_out(number, dy, dm, step):
        slot = ((y + dy) % Y) * 2 + (m_other if dm else m)
        there = (dy - step) % Y
        to = {1: dev_yu, 2: dev_yu2, -1: dev_yd, -2: dev_yd2}[step]
        e_in[(there, dm)] = send(ebuf.at[slot], ebuf.at[slot], es_sem.at[number], er_sem.at[there * 2 + dm], to)

    def e_own():
        arrive(e_in, "mine")
        e_out(2, 0, 0, 1)
        e_out(3, 0, 0, -1)

    def e_ring(k):
        arrive(e_in, (Y - k, 0))
        e_out(4 + 2 * k, Y - k, 0, 1)
        if k < 3:
            arrive(e_in, (k, 0))
            e_out(5 + 2 * k, k, 0, -1)

    def e_other():
        arrive(e_in, "same")
        arrive(e_in, "cross")
        for i, step in enumerate((2, -2, 1, -1)):
            e_out(17 + i, 0, 1, step)

    def e_far():
        arrive(e_in, (2, 1))
        e_out(21, 2, 1, -2)
        e_out(22, 2, 1, -1)
        arrive(e_in, (6, 1))
        e_out(23, 6, 1, 1)

    scale = HD ** (-0.5)

    def head(h):
        cols = slice(h * HD, (h + 1) * HD)
        qh, kh, vh, dh = q_v[:, cols], k_v[:, cols], v_v[:, cols], d_v[:, cols]
        scores = dot(qh, kh, NT) * scale
        scores = jnp.where(valid, scores, NEG_FILL)
        top = jnp.max(scores, axis=-1, keepdims=True)
        expo = jnp.exp(scores - top)
        probs = expo / jnp.sum(expo, axis=-1, keepdims=True)
        dprobs = dot(dh, vh, NT)
        delta = jnp.sum(probs * dprobs, axis=-1, keepdims=True)
        dscore = probs * (dprobs - delta) * scale
        qg_ref[:, cols] = dot(dscore.astype(BF), kh, NN).astype(BF)
        kg[0, :, cols] = dot(dscore.T.astype(BF), qh, NN).astype(BF)

    for copy in loads[1:]:
        copy.wait()
    valid = lax.broadcasted_iota(jnp.int32, (128, 256), 1) < len_ref[0:1, :]
    head(0)
    e_own()
    head(1)
    head(2)
    w_relay(1)
    w_column(1)
    e_ring(1)
    head(3)
    k_pair = send(kg.at[0], kg.at[1], ks_sem.at[0], kr_sem.at[0], dev_s)
    e_other()
    w_relay(3)
    w_column(3)
    e_ring(2)
    w_column(2)
    w_far(1)
    e_ring(3)
    w_far(3)
    e_far()
    w_far(2)

    k_pair.wait_recv()
    for key in list(e_in):
        arrive(e_in, key)

    grads = kg[...].reshape(512, 1024)

    def wg_dot(xt):
        rows = ebuf[pl.ds(xt * Z, Z)].reshape(256, 512)
        part[pl.ds(xt * Z, Z)] = dot(rows, grads, NN).reshape(Z, 64, 1024)

    a_in, b_in, z_in = {}, {}, {}
    x_far = (x + 2) % X

    def a_out(up, k):
        a_send[k] = part[x_far * Z + z_other[k]].astype(BF)
        a_in[k] = send(a_send.at[k], a_recv.at[k], as_sem.at[k], ar_sem.at[k], dev_xu if up else dev_xd)

    def b_out(up, k):
        value = part[(x_up if up else x_down) * Z + z_other[k]]
        if up == k % 2:
            arrive(a_in, k)
            value = value + a_recv[k].astype(F32)
        b_send[up, k] = value.astype(BF)
        b_in[(up, k)] = send(
            b_send.at[up, k], b_recv.at[up, k], bs_sem.at[up * 4 + k], br_sem.at[up * 4 + k],
            dev_xu if up else dev_xd,
        )

    def x_sum(k):
        arrive(b_in, (1, k))
        arrive(b_in, (0, k))
        return part[x * Z + z_other[k]] + b_recv[1, k].astype(F32) + b_recv[0, k].astype(F32)

    def z_out(k):
        z_send[k - 1] = x_sum(k).astype(BF)
        z_in[k] = send(z_send.at[k - 1], z_recv.at[k - 1], zs_sem.at[k - 1], zr_sem.at[k - 1], dev_z[k])

    wg_dot(x_far)
    a_out(1, 3)
    a_out(0, 2)
    wg_dot(x_up)
    b_out(1, 2)
    wg_dot(x_down)
    b_out(0, 3)

    for key in list(w_in):
        arrive(w_in, key)

    def eg_dot(yt):
        rows = wbuf[pl.ds(yt * 2, 2)].reshape(128, 1024)
        term[pl.ds(yt * 2, 2)] = dot(rows, grads, NT).reshape(2, 64, 512)

    t_in = {}

    def t_out(up, k, half):
        yt = (y + k) % Y if up else (y + Y - k) % Y
        value = term[yt * 2 + half]
        first = 4 if half != up else 3
        if k < first:
            arrive(t_in, (up, k + 1, half))
            value = value + e_recv[up, k, half].astype(F32)
        e_send[up, k - 1, half] = value.astype(BF)
        number = (up * 4 + k - 1) * 2 + half
        t_in[(up, k, half)] = send(
            e_send.at[up, k - 1, half], e_recv.at[up, k - 1, half], ts_sem.at[number], tr_sem.at[number],
            dev_yu if up else dev_yd,
        )

    eg_dot((y + 4) % Y)
    t_out(1, 4, 0)
    t_out(0, 4, 1)
    eg_dot((y + 3) % Y)
    t_out(1, 3, 1)
    eg_dot((y + 5) % Y)
    t_out(0, 3, 0)
    b_out(1, 3)
    b_out(0, 2)
    a_out(1, 1)
    a_out(0, 0)
    eg_dot((y + 2) % Y)
    eg_dot((y + 6) % Y)
    t_out(1, 3, 0)
    t_out(0, 3, 1)
    t_out(1, 2, 1)
    t_out(0, 2, 0)
    b_out(1, 0)
    b_out(0, 1)
    eg_dot((y + 1) % Y)
    eg_dot((y + 7) % Y)
    wg_dot(x)
    t_out(1, 2, 0)
    t_out(0, 2, 1)
    z_out(3)
    z_out(2)
    t_out(1, 1, 1)
    t_out(0, 1, 0)
    b_out(1, 1)
    b_out(0, 0)
    eg_dot(y)
    t_out(1, 1, 0)
    t_out(0, 1, 1)

    for up in (1, 0):
        for half in range(2):
            arrive(t_in, (up, 1, half))

    def y_sum(half):
        return term[y * 2 + half] + e_recv[1, 0, half].astype(F32) + e_recv[0, 0, half].astype(F32)

    away = y_sum(m_other).astype(BF)
    e_last[0] = away[:, 0:256]
    e_last[1] = away[:, 256:512]
    l_in = [
        send(e_last.at[0], fin.at[0], ls_sem.at[0], lr_sem.at[0], dev_m),
        send(e_last.at[1], fin.at[1], ls_sem.at[1], lr_sem.at[1], dev_ms),
    ]
    home = y_sum(m)
    e_last[2] = home[:, 256:512].astype(BF)
    l_in.append(send(e_last.at[2], fin.at[2], ls_sem.at[2], lr_sem.at[2], dev_s))

    z_out(1)
    own = x_sum(0)
    for copy in l_in:
        copy.wait_recv()
    enc_sum[c] = home[:, 0:256] + fin[0].astype(F32)
    enc_sum[sister] = fin[1].astype(F32) + fin[2].astype(F32)
    eg_ref[...] = enc_sum[...].reshape(128, 256).T.astype(BF)

    for k in (3, 2, 1):
        arrive(z_in, k)
        own = own + z_recv[k - 1].astype(F32)
    wg_ref[...] = own * (1.0 / 32)

    for copy in sent:
        copy.wait_send()

    @pl.when(inner)
    def _():
        for copy in relayed:
            copy.wait_send()


def shards(queries, keys, values, out_grad, key_weight, encoded, enc_lengths):
    dma = pltpu.SemaphoreType.DMA
    anywhere = pl.BlockSpec(memory_space=pltpu.HBM)
    vmem = pl.BlockSpec(memory_space=pltpu.VMEM)
    held = [
        pltpu.with_memory_space_constraint(array, pltpu.HBM)
        for array in (queries[0], keys[0], values[0], out_grad[0], key_weight[0], encoded)
    ]
    query_grad, encoder_grad, weight_grad = pl.pallas_call(
        kernel,
        out_shape=(
            jax.ShapeDtypeStruct((128, 1024), BF),
            jax.ShapeDtypeStruct((256, 128), BF),
            jax.ShapeDtypeStruct((64, 1024), F32),
        ),
        in_specs=[anywhere] * 7,
        out_specs=(vmem, vmem, vmem),
        scratch_shapes=[
            pltpu.VMEM((128, 1024), BF),
            pltpu.VMEM((256, 1024), BF),
            pltpu.VMEM((256, 1024), BF),
            pltpu.VMEM((128, 1024), BF),
            pltpu.VMEM((256, 128), BF),
            pltpu.VMEM((8, 256), jnp.int32),
            pltpu.VMEM((2, 64, 256), BF),
            pltpu.VMEM((F, 64, 512), BF),
            pltpu.VMEM((F, 64, 1024), BF),
            pltpu.VMEM((2, 256, 1024), BF),
            pltpu.VMEM((F, 64, 512), F32),
            pltpu.VMEM((2, 4, 2, 64, 512), BF),
            pltpu.VMEM((2, 4, 2, 64, 512), BF),
            pltpu.VMEM((3, 64, 256), BF),
            pltpu.VMEM((3, 64, 256), BF),
            pltpu.VMEM((2, 64, 256), F32),
            pltpu.VMEM((F, 64, 1024), F32),
            pltpu.VMEM((4, 64, 1024), BF),
            pltpu.VMEM((4, 64, 1024), BF),
            pltpu.VMEM((2, 4, 64, 1024), BF),
            pltpu.VMEM((2, 4, 64, 1024), BF),
            pltpu.VMEM((3, 64, 1024), BF),
            pltpu.VMEM((3, 64, 1024), BF),
            dma((7,)), dma((21,)), dma((20,)), dma((24,)), dma((17,)), dma((1,)), dma((1,)),
            dma((16,)), dma((16,)), dma((3,)), dma((3,)), dma((4,)), dma((4,)), dma((8,)), dma((8,)),
            dma((3,)), dma((3,)),
        ],
        compiler_params=pltpu.CompilerParams(
            collective_id=0, has_side_effects=True, vmem_limit_bytes=48 * 1024 * 1024
        ),
    )(*held, jnp.broadcast_to(enc_lengths[:, None], (8, 256)))
    return (query_grad[None], encoder_grad, weight_grad[None])


def solution(mesh):
    placed = (
        P("section", "dp", "mp"),
        P("section", "dp", "mp"),
        P("section", "dp", "mp"),
        P("section", "dp", "mp"),
        P("section", "dp", "mp"),
        P("dp", ("section", "mp")),
        P("dp"),
    )
    return jax.shard_map(
        shards,
        mesh=mesh,
        in_specs=placed,
        out_specs=(P("section", "dp", "mp"), P("dp", ("section", "mp")), P("section", "dp", "mp")),
        check_vma=False,
    )
```

time: 82 us -> 65.7 us (0.80)
  Pallas kernels: 71.9 us -> 61.7 us
  local copies, waits for them, and re-layouts: 7.75 us -> 2.04 us
    pallas_call x1, Pallas kernels: 71.9 us -> 61.7 us  [shards(): pl.pallas_call(kernel, out_shape=(jax.ShapeDtypeStruct((128, 1024), BF),...]
    unnamed x15 -> x3, local copies, waits for them, and re-layouts: 7.75 us -> 2.04 us
where the time goes in v2:
time: 65.7 us; the launch traced here: 65.1 us
  Pallas kernels  61.7 us (94%)
  local copies, waits for them, and re-layouts  2.04 us (3%)
  between operations  1.29 us (2%)
    pallas_call x1, Pallas kernels, shards(): pl.pallas_call(kernel, out_shape=(jax.ShapeDtypeStruct((128, 1024), BF),...  61.7 us
    unnamed x3, local copies, waits for them, and re-layouts  2.04 us

profile of v2, /device:TPU:1, one launch (start us, length us, event | category | flops | bytes accessed | tf_op | source)
XLA Modules:
  0.0 65.1 jit_solution(8692249113141096757)
XLA Ops:
  1.3 61.7 %shard_map.94 = (bf16[128,1024]{1,0:T(8,128)(2,1)S(1)}, bf16[256,128]{1,0:T(8,128)(2,1)S(1)}, f32[64,1024]{1,0:T(8,128)S(1)}) custom-call(bf16[128,1024]{1,0:T(8,128)(2,1)} %bitcast.13, bf16[256,1024]{1,0:T(8,128)(2,1)} %bitcast.11, bf16[256,1024]{1,0:T(8,128)(2,1)} %bitcast.12, bf16[128,1024]{1,0:T(8,128)(2,1)} %bitcast.14, bf16[64,1024]{1,0:T(8,128)(2,1)} %bitcast.15, ...), custom_call_target="tpu_custom_call" | custom-call | tf_op jit(solution)/shard_map/pallas_call | solution.py:357
  63.0 0.7 %copy.14 = bf16[1,128,1024]{2,1,0:T(8,128)(2,1)} copy(bf16[1,128,1024]{2,1,0:T(8,128)(2,1)S(1)} %bitcast.10) | data formatting | bytes 524288
  63.7 0.6 copy.15
  64.4 0.7 %copy.16 = f32[1,64,1024]{2,1,0:T(8,128)} copy(f32[1,64,1024]{2,1,0:T(8,128)S(1)} %bitcast.9) | data formatting | bytes 524288
  (1 shorter events, 0.0 us)

commit v3 on v0

v3 whole, which is shorter than its diff:
```python
import jax
import jax.numpy as jnp
from jax import lax
from jax.experimental import pallas as pl
from jax.experimental.pallas import tpu as pltpu
from jax.sharding import PartitionSpec as P

HD = 256
NEG_FILL = -1e30
X, Z, Y = 4, 4, 8
F = X * Z
MESH = pl.DeviceIdType.MESH
BF = jnp.bfloat16
F32 = jnp.float32

NT = (((1,), (1,)), ((), ()))
NN = (((1,), (0,)), ((), ()))
TN = (((0,), (0,)), ((), ()))


def dot(a, b, dims):
    return lax.dot_general(a, b, dims, preferred_element_type=F32)


def kernel(
    q_hbm, k_hbm, v_hbm, d_hbm, w_hbm, enc_hbm, len_hbm,
    qg_ref, eg_ref, wg_ref,
    q_v, k_v, v_v, d_v, enc_v, len_v, et, ebuf, wbuf, kg,
    term, t_send, t_recv, l_send, l_recv, enc_sum,
    part, a_send, a_recv, b_send, b_recv, z_send, z_recv,
    loc_sem, ws_sem, wr_sem, es_sem, er_sem, ks_sem, kr_sem,
    ts_sem, tr_sem, ls_sem, lr_sem, as_sem, ar_sem, bs_sem, br_sem, zs_sem, zr_sem,
):
    dp = lax.axis_index("dp")
    y = lax.axis_index("section")
    m = lax.axis_index("mp")
    x = dp // 8
    z = (dp // 2) % 4
    c = dp % 2
    q = z % 2
    f = dp // 2

    def dev(x=x, z=z, c=c, y=y, m=m):
        return {"dp": x * 8 + z * 2 + c, "section": y, "mp": m}

    z_other = [z, z + 1 - 2 * q, (z + 2) % Z, Z - 1 - z]
    sister, m_other = 1 - c, 1 - m
    dev_x = [dev(x=(x + dx) % X) for dx in range(X)]
    dev_y = {step: dev(y=(y + Y + step) % Y) for step in (1, -1, 2, -2)}
    dev_z = [dev(z=other) for other in z_other]
    group = [dict(), dict(c=sister), dict(z=z_other[1]), dict(c=sister, z=z_other[1])]
    quarter = [c * 2 + q, sister * 2 + q, c * 2 + 1 - q, sister * 2 + 1 - q]
    dev_home = [dev(**other) for other in group]
    dev_away = [dev(m=m_other, **other) for other in group]

    loads = [
        pltpu.make_async_copy(src, dst, loc_sem.at[i])
        for i, (src, dst) in enumerate(
            [(enc_hbm, enc_v), (q_hbm, q_v), (k_hbm, k_v), (d_hbm, d_v), (v_hbm, v_v),
             (w_hbm.at[pl.ds(pl.multiple_of(q * 32, 32), 32)], wbuf.at[f]), (len_hbm, len_v)]
        )
    ]

    partners = dev_x[1:] + list(dev_y.values()) + dev_z[2:] + dev_home[1:] + dev_away
    barrier = pltpu.get_barrier_semaphore()
    for partner in partners:
        pl.semaphore_signal(barrier, inc=1, device_id=partner, device_id_type=MESH)
    for copy in loads:
        copy.start()
    loads[0].wait()
    et[...] = enc_v[...].astype(F32).T.astype(BF).reshape(4, 32, 256)
    ebuf[y, m, :, 0:256] = et[quarter[0]]
    pl.semaphore_wait(barrier, len(partners))

    sent = []

    def send(src, dst, ssem, rsem, device):
        copy = pltpu.make_async_remote_copy(
            src_ref=src, dst_ref=dst, send_sem=ssem, recv_sem=rsem, device_id=device, device_id_type=MESH
        )
        copy.start()
        sent.append(copy)
        return copy

    arrived = set()

    def arrive(inward, key):
        if (id(inward), key) not in arrived:
            arrived.add((id(inward), key))
            inward[key].wait_recv()

    e_in, w_in, k_in = {}, {}, {}

    def e_piece(across, j):
        number = 18 + across * 4 + j
        e_in[("piece", across, j)] = send(
            et.at[quarter[j]], ebuf.at[y, m, :, pl.ds(j * 256, 256)], es_sem.at[number], er_sem.at[number],
            dev_away[j] if across else dev_home[j],
        )

    def w_send(src, dst, dx, k, to):
        number = dx * 4 + k
        w_in[(dx, k)] = send(src, dst, ws_sem.at[number], wr_sem.at[number], to)

    def w_rows(half):
        return w_hbm.at[pl.ds(pl.multiple_of(half * 32, 32), 32)]

    def w_own():
        w_own_z()
        w_own_x()

    def w_own_z():
        for k in (1, 3, 2):
            w_send(w_rows(q if k == 2 else 1 - q), wbuf.at[f], 0, k, dev_z[k])

    def w_own_x():
        for dx in (1, 3, 2):
            w_send(w_rows(q), wbuf.at[f], X - dx, 0, dev_x[dx])

    def w_column(k):
        arrive(w_in, (0, k))
        slot = wbuf.at[x * Z + z_other[k]]
        for dx in (1, 3, 2):
            w_send(slot, slot, X - dx, k, dev_x[dx])

    def e_out(dm, dy, step, rows=None, number=None):
        slot = ebuf.at[(y + dy) % Y, m_other if dm else m]
        if rows is not None:
            slot = slot.at[pl.ds(rows, 16)]
        there = (dy - step) % Y
        if number is None:
            number = there
        e_in[(dm, number)] = send(
            slot, slot, es_sem.at[dm * 9 + number], er_sem.at[dm * 9 + number], dev_y[step]
        )

    def e_first(dm):
        for j in range(1 - dm, 4):
            arrive(e_in, ("piece", dm, j))
        e_out(dm, 0, 2)
        e_out(dm, 0, -2)

    def e_near(dm):
        e_out(dm, 0, 1)
        e_out(dm, 0, -1)

    def e_far(dm):
        arrive(e_in, (dm, 6))
        e_out(dm, 6, 2, 0, 4)
        e_out(dm, 6, 1)
        arrive(e_in, (dm, 2))
        e_out(dm, 2, -2, 16, 8)
        e_out(dm, 2, -1)

    def e_all(dm):
        for number in (1, 7, 2, 6, 3, 5, 4, 8):
            arrive(e_in, (dm, number))

    scale = HD ** (-0.5)

    def head(h):
        cols = slice(h * HD, (h + 1) * HD)
        qh, kh, vh, dh = q_v[:, cols], k_v[:, cols], v_v[:, cols], d_v[:, cols]
        scores = dot(qh, kh, NT) * scale
        scores = jnp.where(valid, scores, NEG_FILL)
        top = jnp.max(scores, axis=-1, keepdims=True)
        expo = jnp.exp(scores - top)
        probs = expo / jnp.sum(expo, axis=-1, keepdims=True)
        dprobs = dot(dh, vh, NT)
        delta = jnp.sum(probs * dprobs, axis=-1, keepdims=True)
        dscore = probs * (dprobs - delta) * scale
        kg[0, :, cols] = dot(dscore.T.astype(BF), qh, NN).astype(BF)
        k_send(2, h, 0, 2)
        k_send(1, h, 0, 1)
        qg_ref[:, cols] = dot(dscore.astype(BF), kh, NN).astype(BF)

    def k_send(j, h, src, to):
        cols = pl.ds(h * HD, HD)
        number = (j - 1) * 4 + h
        k_in[(j, h)] = send(
            kg.at[src, :, cols], kg.at[j, :, cols], ks_sem.at[number], kr_sem.at[number], dev_home[to]
        )

    def k_relay(h):
        arrive(k_in, (2, h))
        k_send(3, h, 2, 1)

    def eg_dot(t):
        grads = kg[2 * t : 2 * t + 2].reshape(512, 1024)
        term[t] = dot(wbuf[...].reshape(512, 1024), grads, NT).reshape(F, 32, 512)

    t_in = {}

    def t_out(t, up, k, half):
        yt = (y + k) % Y if up else (y + Y - k) % Y
        value = term[t, yt * 2 + half]
        if k < 3:
            arrive(t_in, (t, up, k + 1, half))
            value = value + t_recv[t, up, k, half].astype(F32)
        if k == 2 and half != up:
            arrive(t_in, (t, up, 4, half))
            value = value + t_recv[t, up, 3, half].astype(F32)
        t_send[t, up, k - 1, half] = value.astype(BF)
        number = ((t * 2 + up) * 4 + k - 1) * 2 + half
        step = 2 if k == 4 else 1
        t_in[(t, up, k, half)] = send(
            t_send.at[t, up, k - 1, half], t_recv.at[t, up, k - 1, half], ts_sem.at[number], tr_sem.at[number],
            dev_y[step if up else -step],
        )

    def eg_start(t):
        t_out(t, 1, 4, 0)
        t_out(t, 0, 4, 1)
        eg_step(t, 3)

    def eg_step(t, k):
        t_out(t, 1, k, 0)
        t_out(t, 0, k, 1)
        t_out(t, 1, k, 1)
        t_out(t, 0, k, 0)

    l_in = {}
    home = {}

    def l_out(across, j, value):
        number = across * 4 + j
        l_send[number] = value.astype(BF)
        l_in[(across, j)] = send(
            l_send.at[number], l_recv.at[number], ls_sem.at[number], lr_sem.at[number],
            dev_away[j] if across else dev_home[j],
        )

    def y_sum(t, half):
        return term[t, y * 2 + half] + t_recv[t, 1, 0, half].astype(F32) + t_recv[t, 0, 0, half].astype(F32)

    def eg_end(t):
        for up in (1, 0):
            for half in range(2):
                arrive(t_in, (t, up, 1, half))
        away = y_sum(t, m_other)
        l_out(1, 2 * t, away[:, 0:256])
        l_out(1, 2 * t + 1, away[:, 256:512])
        total = y_sum(t, m)
        if t == 0:
            home[0] = total[:, 0:256]
        else:
            l_out(0, 2, total[:, 0:256])
        l_out(0, 2 * t + 1, total[:, 256:512])

    first = (q + m) % 2

    def bit(turn):
        return 1 - first if turn else first

    def place(dx, turn, b):
        other = (z + 2 * b) % Z + bit(turn) * (1 - 2 * q)
        return ((x + dx) % X) * 2 + other // 2, other % 2

    def wg_dot(mt):
        rows = ebuf[:, mt].reshape(256, 1024)
        part[:, mt] = dot(rows, kg[...].reshape(1024, 1024), NN).reshape(Y, 32, 1024)

    a_in, b_in = {}, {}

    def a_out(turn, b):
        number = turn * 2 + b
        a_send[number] = part[place(2, turn, b)].astype(BF)
        a_in[number] = send(
            a_send.at[number], a_recv.at[number], as_sem.at[number], ar_sem.at[number], dev_x[1 if b else 3]
        )

    def b_out(turn, b, up):
        number = turn * 2 + b
        value = part[place(1 if up else 3, turn, b)]
        if up == b:
            arrive(a_in, number)
            value = value + a_recv[number].astype(F32)
        slot = up * 4 + number
        b_send[slot] = value.astype(BF)
        b_in[(number, up)] = send(
            b_send.at[slot], b_recv.at[slot], bs_sem.at[slot], br_sem.at[slot], dev_x[1 if up else 3]
        )

    def wg_start(turn):
        a_out(turn, 1)
        a_out(turn, 0)
        b_out(turn, 0, 1)
        b_out(turn, 1, 0)

    def wg_next(turn):
        b_out(turn, 1, 1)
        b_out(turn, 0, 0)

    def x_sum(turn, b, zt):
        number = turn * 2 + b
        return (
            part[x * 2 + zt // 2, zt % 2] + b_recv[number].astype(F32) + b_recv[4 + number].astype(F32)
        )

    def z_copy(k):
        return pltpu.make_async_remote_copy(
            src_ref=z_send.at[k - 1], dst_ref=z_recv.at[k - 1], send_sem=zs_sem.at[k - 1], recv_sem=zr_sem.at[k - 1],
            device_id=dev_z[k], device_id_type=MESH,
        )

    def z_out(turn):
        for up in (1, 0):
            arrive(b_in, (turn * 2 + 1, up))
        k = 2 + bit(turn)
        zt = (z + 2) % Z + bit(turn) * (1 - 2 * q)
        z_send[k - 1] = x_sum(turn, 1, zt).astype(BF)
        send(z_send.at[k - 1], z_recv.at[k - 1], zs_sem.at[k - 1], zr_sem.at[k - 1], dev(z=zt))

    def z_last():
        for turn in (0, 1):
            for up in (1, 0):
                arrive(b_in, (turn * 2, up))
        z_send[0] = x_sum(1 - first, 0, z_other[1]).astype(BF)
        send(z_send.at[0], z_recv.at[0], zs_sem.at[0], zr_sem.at[0], dev_z[1])

    for j in (2, 3, 0, 1):
        e_piece(1, j)
    for j in (2, 3, 1):
        e_piece(0, j)
    w_own()
    for copy in loads[1:]:
        copy.wait()
    valid = lax.broadcasted_iota(jnp.int32, (128, 256), 1) < len_v[0:1, :]
    head(0)
    head(1)
    e_first(0)
    e_near(0)
    head(2)
    head(3)
    w_column(1)
    w_column(3)
    e_first(1)
    w_column(2)
    k_relay(0)
    e_far(0)
    e_near(1)
    k_relay(1)
    e_far(1)
    k_relay(2)
    for key in list(w_in):
        arrive(w_in, key)
    for h in range(4):
        arrive(k_in, (1, h))
    eg_dot(0)
    eg_start(0)
    k_relay(3)
    for key in list(k_in):
        arrive(k_in, key)
    eg_dot(1)
    eg_start(1)
    eg_step(0, 2)
    e_all(0)
    wg_dot(m)
    wg_start(0)
    eg_step(1, 2)
    e_all(1)
    wg_dot(m_other)
    wg_start(1)
    eg_step(0, 1)
    wg_next(0)
    eg_step(1, 1)
    eg_end(0)
    wg_next(1)
    eg_end(1)
    z_out(0)
    z_out(1)
    z_last()

    own = x_sum(first, 0, z)
    z_copy(2).wait_recv()
    wg_ref[pl.ds(pl.multiple_of(q * 32, 32), 32), :] = (own + z_recv[1].astype(F32)) * (1.0 / 32)
    z_copy(1).wait_recv()
    z_copy(3).wait_recv()
    wg_ref[pl.ds(pl.multiple_of((1 - q) * 32, 32), 32), :] = (
        z_recv[0].astype(F32) + z_recv[2].astype(F32)
    ) * (1.0 / 32)

    for key in list(l_in):
        arrive(l_in, key)
    for j in range(4):
        here = home[0] if j == 0 else l_recv[j].astype(F32)
        enc_sum[quarter[j]] = here + l_recv[4 + j].astype(F32)
    eg_ref[...] = enc_sum[...].reshape(128, 256).T.astype(BF)

    for copy in sent:
        copy.wait_send()


def write_out(a, b, c, a_out, b_out, c_out, sems):
    copies = [
        pltpu.make_async_copy(src, dst, sems.at[i])
        for i, (src, dst) in enumerate([(a, a_out), (b, b_out), (c, c_out)])
    ]
    for copy in copies:
        copy.start()
    for copy in copies:
        copy.wait()


def shards(queries, keys, values, out_grad, key_weight, encoded, enc_lengths):
    dma = pltpu.SemaphoreType.DMA
    anywhere = pl.BlockSpec(memory_space=pltpu.HBM)
    vmem = pl.BlockSpec(memory_space=pltpu.VMEM)
    held = [
        pltpu.with_memory_space_constraint(array, pltpu.HBM)
        for array in (queries[0], keys[0], values[0], out_grad[0], key_weight[0], encoded)
    ]
    query_grad, encoder_grad, weight_grad = pl.pallas_call(
        kernel,
        out_shape=(
            jax.ShapeDtypeStruct((128, 1024), BF),
            jax.ShapeDtypeStruct((256, 128), BF),
            jax.ShapeDtypeStruct((64, 1024), F32),
        ),
        in_specs=[anywhere] * 7,
        out_specs=(vmem, vmem, vmem),
        scratch_shapes=[
            pltpu.VMEM((128, 1024), BF),
            pltpu.VMEM((256, 1024), BF),
            pltpu.VMEM((256, 1024), BF),
            pltpu.VMEM((128, 1024), BF),
            pltpu.VMEM((256, 128), BF),
            pltpu.VMEM((8, 256), jnp.int32),
            pltpu.VMEM((4, 32, 256), BF),
            pltpu.VMEM((Y, 2, 32, 1024), BF),
            pltpu.VMEM((F, 32, 1024), BF),
            pltpu.VMEM((4, 256, 1024), BF),
            pltpu.VMEM((2, F, 32, 512), F32),
            pltpu.VMEM((2, 2, 4, 2, 32, 512), BF),
            pltpu.VMEM((2, 2, 4, 2, 32, 512), BF),
            pltpu.VMEM((8, 32, 256), BF),
            pltpu.VMEM((8, 32, 256), BF),
            pltpu.VMEM((4, 32, 256), F32),
            pltpu.VMEM((Y, 2, 32, 1024), F32),
            pltpu.VMEM((4, 32, 1024), BF),
            pltpu.VMEM((4, 32, 1024), BF),
            pltpu.VMEM((8, 32, 1024), BF),
            pltpu.VMEM((8, 32, 1024), BF),
            pltpu.VMEM((3, 32, 1024), BF),
            pltpu.VMEM((3, 32, 1024), BF),
            dma((7,)), dma((16,)), dma((16,)), dma((26,)), dma((26,)), dma((12,)), dma((12,)),
            dma((32,)), dma((32,)), dma((8,)), dma((8,)), dma((4,)), dma((4,)), dma((8,)), dma((8,)), dma((3,)), dma((3,)),
        ],
        compiler_params=pltpu.CompilerParams(
            collective_id=0, has_side_effects=True, vmem_limit_bytes=48 * 1024 * 1024
        ),
    )(*held, jnp.broadcast_to(enc_lengths[:, None], (8, 256)))
    results = tuple(
        pltpu.with_memory_space_constraint(array, pltpu.VMEM) for array in (query_grad, encoder_grad, weight_grad)
    )
    query_grad, encoder_grad, weight_grad = pl.pallas_call(
        write_out,
        out_shape=tuple(jax.ShapeDtypeStruct(array.shape, array.dtype) for array in results),
        in_specs=[pl.BlockSpec(memory_space=pl.ANY)] * 3,
        out_specs=(pl.BlockSpec(memory_space=pltpu.HBM),) * 3,
        scratch_shapes=[dma((3,))],
    )(*results)
    return (query_grad[None], encoder_grad, weight_grad[None])


def solution(mesh):
    placed = (
        P("section", "dp", "mp"),
        P("section", "dp", "mp"),
        P("section", "dp", "mp"),
        P("section", "dp", "mp"),
        P("section", "dp", "mp"),
        P("dp", ("section", "mp")),
        P("dp"),
    )
    return jax.shard_map(
        shards,
        mesh=mesh,
        in_specs=placed,
        out_specs=(P("section", "dp", "mp"), P("dp", ("section", "mp")), P("section", "dp", "mp")),
        check_vma=False,
    )
```

time: 462 us -> 59.8 us (0.13)
  waiting for transfers between devices: 405 us -> 0 us
  Pallas kernels: 0 us -> 58.4 us
  between operations: 14.5 us -> 1.29 us
  local copies, waits for them, and re-layouts: 12.6 us -> 0.01 us
  matrix products: 10.8 us -> 0 us
  starting transfers between devices: 9.43 us -> 0 us
  other arithmetic: 5.41 us -> 0 us
    reduce_scatter x1 -> x0, waiting for transfers between devices: 208 us -> none  [shards(): lax.psum_scatter(term, ('section', 'mp'), scatter_dimension=1, tiled=True)]
    all_gather x2 -> x0, waiting for transfers between devices: 183 us -> none  [the longest x1 93.4 us: shards(): lax.all_gather(weight_rows, 'dp', axis=0, tiled=True)]
    pallas_call x0 -> x2, Pallas kernels: none -> 58.4 us  [the longest x1 57.5 us: shards(): pl.pallas_call(kernel, out_shape=(jax.ShapeDtypeStruct((128, 1024), BF),...]
    all_to_all x1 -> x0, waiting for transfers between devices: 12.3 us -> none  [shards(): lax.all_to_all(bucket, 'dp', split_axis=0, concat_axis=0, tiled=True)]
    dot_general x5 -> x0, matrix products: 10.3 us -> none  [the longest x1 4.85 us: shards(): jnp.dot(key_grad, lax.all_gather(weight_rows, 'dp', axis=0, tiled=True).T...]
    all_to_all x1 -> x0, starting transfers between devices: 9.32 us -> none  [shards(): lax.all_to_all(bucket, 'dp', split_axis=0, concat_axis=0, tiled=True)]
    convert_element_type x2 -> x0, local copies, waits for them, and re-layouts: 6.57 us -> none  [the longest x1 6.4 us: shards(): partial_grad.astype(jnp.bfloat16)]
    another operation x4 -> x0, local copies, waits for them, and re-layouts: 5.14 us -> none  [the longest x1 1.44 us: group_back(): k_group = k.reshape(enc_rows, group, HD)]
  transfers between devices with their start and end apart: 4 -> 0, of which waited for: 4 -> 0; matrix products, arithmetic and copies ran while one was open for 6% -> 0% of each run, Pallas kernels for 0% -> 0%
where the time goes in v3:
time: 59.8 us; the launch traced here: 59.7 us
  Pallas kernels  58.4 us (98%)
  between operations  1.29 us (2%)
    pallas_call x1, Pallas kernels, shards(): pl.pallas_call(kernel, out_shape=(jax.ShapeDtypeStruct((128, 1024), BF),...  57.5 us

profile of v3, /device:TPU:1, one launch (start us, length us, event | category | flops | bytes accessed | tf_op | source)
XLA Modules:
  0.0 59.7 jit_solution(18004363825601648758)
XLA Ops:
  1.3 57.5 %shard_map.94 = (bf16[128,1024]{1,0:T(8,128)(2,1)S(1)}, bf16[256,128]{1,0:T(8,128)(2,1)S(1)}, f32[64,1024]{1,0:T(8,128)S(1)}) custom-call(bf16[128,1024]{1,0:T(8,128)(2,1)} %bitcast.11, bf16[256,1024]{1,0:T(8,128)(2,1)} %bitcast.9, bf16[256,1024]{1,0:T(8,128)(2,1)} %bitcast.10, bf16[128,1024]{1,0:T(8,128)(2,1)} %bitcast.12, bf16[64,1024]{1,0:T(8,128)(2,1)} %bitcast.13, ...), custom_call_target="tpu_custom_call" | custom-call | tf_op jit(solution)/shard_map/pallas_call | solution.py:413
  58.8 0.8 %shard_map.95 = (bf16[128,1024]{1,0:T(8,128)(2,1)}, bf16[256,128]{1,0:T(8,128)(2,1)}, f32[64,1024]{1,0:T(8,128)}) custom-call(bf16[128,1024]{1,0:T(8,128)(2,1)S(1)} %get-tuple-element.9.a, bf16[256,128]{1,0:T(8,128)(2,1)S(1)} %get-tuple-element.10.b, f32[64,1024]{1,0:T(8,128)S(1)} %get-tuple-element.11.c), custom_call_target="tpu_custom_call" | custom-call | tf_op jit(solution)/shard_map/pallas_call | solution.py:456
  (1 shorter events, 0.0 us)

commit v4 on v3

--- a/solution.py
+++ b/solution.py
@@ -27,9 +27,9 @@
     qg_ref, eg_ref, wg_ref,
     q_v, k_v, v_v, d_v, enc_v, len_v, et, ebuf, wbuf, kg,
     term, t_send, t_recv, l_send, l_recv, enc_sum,
-    part, a_send, a_recv, b_send, b_recv, z_send, z_recv,
+    part, b_send, b_recv, z_send, z_recv,
     loc_sem, ws_sem, wr_sem, es_sem, er_sem, ks_sem, kr_sem,
-    ts_sem, tr_sem, ls_sem, lr_sem, as_sem, ar_sem, bs_sem, br_sem, zs_sem, zr_sem,
+    ts_sem, tr_sem, ls_sem, lr_sem, bs_sem, br_sem, zs_sem, zr_sem,
 ):
     dp = lax.axis_index("dp")
     y = lax.axis_index("section")
@@ -61,12 +61,13 @@
         )
     ]
 
+    for copy in loads:
+        copy.start()
+
     partners = dev_x[1:] + list(dev_y.values()) + dev_z[2:] + dev_home[1:] + dev_away
     barrier = pltpu.get_barrier_semaphore()
     for partner in partners:
         pl.semaphore_signal(barrier, inc=1, device_id=partner, device_id_type=MESH)
-    for copy in loads:
-        copy.start()
     loads[0].wait()
     et[...] = enc_v[...].astype(F32).T.astype(BF).reshape(4, 32, 256)
     ebuf[y, m, :, 0:256] = et[quarter[0]]
@@ -260,42 +261,26 @@
         rows = ebuf[:, mt].reshape(256, 1024)
         part[:, mt] = dot(rows, kg[...].reshape(1024, 1024), NN).reshape(Y, 32, 1024)
 
-    a_in, b_in = {}, {}
-
-    def a_out(turn, b):
+    b_in = {}
+
+    def b_out(turn, b, dx):
         number = turn * 2 + b
-        a_send[number] = part[place(2, turn, b)].astype(BF)
-        a_in[number] = send(
-            a_send.at[number], a_recv.at[number], as_sem.at[number], ar_sem.at[number], dev_x[1 if b else 3]
-        )
-
-    def b_out(turn, b, up):
-        number = turn * 2 + b
-        value = part[place(1 if up else 3, turn, b)]
-        if up == b:
-            arrive(a_in, number)
-            value = value + a_recv[number].astype(F32)
-        slot = up * 4 + number
-        b_send[slot] = value.astype(BF)
-        b_in[(number, up)] = send(
-            b_send.at[slot], b_recv.at[slot], bs_sem.at[slot], br_sem.at[slot], dev_x[1 if up else 3]
+        slot = (X - dx - 1) * 4 + number
+        b_send[slot] = part[place(dx, turn, b)].astype(BF)
+        b_in[(number, X - dx)] = send(
+            b_send.at[slot], b_recv.at[slot], bs_sem.at[slot], br_sem.at[slot], dev_x[dx]
         )
 
     def wg_start(turn):
-        a_out(turn, 1)
-        a_out(turn, 0)
-        b_out(turn, 0, 1)
-        b_out(turn, 1, 0)
-
-    def wg_next(turn):
-        b_out(turn, 1, 1)
-        b_out(turn, 0, 0)
+        for b in (1, 0):
+            for dx in (2, 1, 3):
+                b_out(turn, b, dx)
 
     def x_sum(turn, b, zt):
-        number = turn * 2 + b
-        return (
-            part[x * 2 + zt // 2, zt % 2] + b_recv[number].astype(F32) + b_recv[4 + number].astype(F32)
-        )
+        value = part[x * 2 + zt // 2, zt % 2]
+        for dx in (1, 2, 3):
+            value = value + b_recv[(dx - 1) * 4 + turn * 2 + b].astype(F32)
+        return value
 
     def z_copy(k):
         return pltpu.make_async_remote_copy(
@@ -304,8 +289,8 @@
         )
 
     def z_out(turn):
-        for up in (1, 0):
-            arrive(b_in, (turn * 2 + 1, up))
+        for dx in (1, 3, 2):
+            arrive(b_in, (turn * 2 + 1, dx))
         k = 2 + bit(turn)
         zt = (z + 2) % Z + bit(turn) * (1 - 2 * q)
         z_send[k - 1] = x_sum(turn, 1, zt).astype(BF)
@@ -313,8 +298,8 @@
 
     def z_last():
         for turn in (0, 1):
-            for up in (1, 0):
-                arrive(b_in, (turn * 2, up))
+            for dx in (1, 3, 2):
+                arrive(b_in, (turn * 2, dx))
         z_send[0] = x_sum(1 - first, 0, z_other[1]).astype(BF)
         send(z_send.at[0], z_recv.at[0], zs_sem.at[0], zr_sem.at[0], dev_z[1])
 
@@ -353,21 +338,19 @@
         arrive(k_in, key)
     eg_dot(1)
     eg_start(1)
-    eg_step(0, 2)
     e_all(0)
     wg_dot(m)
     wg_start(0)
-    eg_step(1, 2)
+    eg_step(0, 2)
     e_all(1)
     wg_dot(m_other)
     wg_start(1)
+    eg_step(1, 2)
     eg_step(0, 1)
-    wg_next(0)
+    z_out(0)
     eg_step(1, 1)
     eg_end(0)
-    wg_next(1)
     eg_end(1)
-    z_out(0)
     z_out(1)
     z_last()
 
@@ -437,14 +420,12 @@
             pltpu.VMEM((8, 32, 256), BF),
             pltpu.VMEM((4, 32, 256), F32),
             pltpu.VMEM((Y, 2, 32, 1024), F32),
-            pltpu.VMEM((4, 32, 1024), BF),
-            pltpu.VMEM((4, 32, 1024), BF),
-            pltpu.VMEM((8, 32, 1024), BF),
-            pltpu.VMEM((8, 32, 1024), BF),
+            pltpu.VMEM((12, 32, 1024), BF),
+            pltpu.VMEM((12, 32, 1024), BF),
             pltpu.VMEM((3, 32, 1024), BF),
             pltpu.VMEM((3, 32, 1024), BF),
             dma((7,)), dma((16,)), dma((16,)), dma((26,)), dma((26,)), dma((12,)), dma((12,)),
-            dma((32,)), dma((32,)), dma((8,)), dma((8,)), dma((4,)), dma((4,)), dma((8,)), dma((8,)), dma((3,)), dma((3,)),
+            dma((32,)), dma((32,)), dma((8,)), dma((8,)), dma((12,)), dma((12,)), dma((3,)), dma((3,)),
         ],
         compiler_params=pltpu.CompilerParams(
             collective_id=0, has_side_effects=True, vmem_limit_bytes=48 * 1024 * 1024

time: 59.8 us -> 56.6 us (0.946)
  Pallas kernels: 58.4 us -> 55.1 us
    pallas_call x1, Pallas kernels: 57.5 us -> 54.3 us  [shards(): pl.pallas_call(kernel, out_shape=(jax.ShapeDtypeStruct((128, 1024), BF),...]
where the time goes in v4:
time: 56.6 us; the launch traced here: 56.4 us
  Pallas kernels  55.1 us (97%)
  between operations  1.29 us (2%)
    pallas_call x1, Pallas kernels, shards(): pl.pallas_call(kernel, out_shape=(jax.ShapeDtypeStruct((128, 1024), BF),...  54.3 us

profile of v4, /device:TPU:1, one launch (start us, length us, event | category | flops | bytes accessed | tf_op | source)
XLA Modules:
  0.0 56.4 jit_solution(3631804878029314420)
XLA Ops:
  1.3 54.3 %shard_map.94 = (bf16[128,1024]{1,0:T(8,128)(2,1)S(1)}, bf16[256,128]{1,0:T(8,128)(2,1)S(1)}, f32[64,1024]{1,0:T(8,128)S(1)}) custom-call(bf16[128,1024]{1,0:T(8,128)(2,1)} %bitcast.11, bf16[256,1024]{1,0:T(8,128)(2,1)} %bitcast.9, bf16[256,1024]{1,0:T(8,128)(2,1)} %bitcast.10, bf16[128,1024]{1,0:T(8,128)(2,1)} %bitcast.12, bf16[64,1024]{1,0:T(8,128)(2,1)} %bitcast.13, ...), custom_call_target="tpu_custom_call" | custom-call | tf_op jit(solution)/shard_map/pallas_call | solution.py:396
  55.6 0.8 %shard_map.95 = (bf16[128,1024]{1,0:T(8,128)(2,1)}, bf16[256,128]{1,0:T(8,128)(2,1)}, f32[64,1024]{1,0:T(8,128)}) custom-call(bf16[128,1024]{1,0:T(8,128)(2,1)S(1)} %get-tuple-element.9.a, bf16[256,128]{1,0:T(8,128)(2,1)S(1)} %get-tuple-element.10.b, f32[64,1024]{1,0:T(8,128)S(1)} %get-tuple-element.11.c), custom_call_target="tpu_custom_call" | custom-call | tf_op jit(solution)/shard_map/pallas_call | solution.py:437
  (1 shorter events, 0.0 us)

commit v5 on v4

--- a/solution.py
+++ b/solution.py
@@ -323,8 +323,8 @@
     w_column(2)
     k_relay(0)
     e_far(0)
+    k_relay(1)
     e_near(1)
-    k_relay(1)
     e_far(1)
     k_relay(2)
     for key in list(w_in):

time: 56.6 us -> 56.6 us (level)
  no operation moved by 1% of the time
where the time goes in v5:
time: 56.6 us; the launch traced here: 56.5 us
  Pallas kernels  55.2 us (98%)
  between operations  1.29 us (2%)
    pallas_call x1, Pallas kernels, shards(): pl.pallas_call(kernel, out_shape=(jax.ShapeDtypeStruct((128, 1024), BF),...  54.4 us

profile of v5, /device:TPU:1, one launch (start us, length us, event | category | flops | bytes accessed | tf_op | source)
XLA Modules:
  0.0 56.5 jit_solution(10062624602834738676)
XLA Ops:
  1.3 54.4 %shard_map.94 = (bf16[128,1024]{1,0:T(8,128)(2,1)S(1)}, bf16[256,128]{1,0:T(8,128)(2,1)S(1)}, f32[64,1024]{1,0:T(8,128)S(1)}) custom-call(bf16[128,1024]{1,0:T(8,128)(2,1)} %bitcast.11, bf16[256,1024]{1,0:T(8,128)(2,1)} %bitcast.9, bf16[256,1024]{1,0:T(8,128)(2,1)} %bitcast.10, bf16[128,1024]{1,0:T(8,128)(2,1)} %bitcast.12, bf16[64,1024]{1,0:T(8,128)(2,1)} %bitcast.13, ...), custom_call_target="tpu_custom_call" | custom-call | tf_op jit(solution)/shard_map/pallas_call | solution.py:396
  55.7 0.8 %shard_map.95 = (bf16[128,1024]{1,0:T(8,128)(2,1)}, bf16[256,128]{1,0:T(8,128)(2,1)}, f32[64,1024]{1,0:T(8,128)}) custom-call(bf16[128,1024]{1,0:T(8,128)(2,1)S(1)} %get-tuple-element.9.a, bf16[256,128]{1,0:T(8,128)(2,1)S(1)} %get-tuple-element.10.b, f32[64,1024]{1,0:T(8,128)S(1)} %get-tuple-element.11.c), custom_call_target="tpu_custom_call" | custom-call | tf_op jit(solution)/shard_map/pallas_call | solution.py:437
  (1 shorter events, 0.0 us)
